TPU v7x, 32 devices: a whole 2x2x4 slice. The times are simulated.
32 devices in a mesh: seq: 8 (over y, x, core), tensor: 4 (over z).
Axes of the slice: x: 2, y: 2, z: 4, core: 2. Of those that a mesh axis runs over, the one named last changes fastest.
Arguments:
- hidden: bfloat16 [8192, 3072], P('seq', 'tensor'), may hold values from -6 to 6
- norm_gain: float32 [3072], replicated, may hold values from 0.1 to 1.9
- query_weight: bfloat16 [3072, 4096], P(None, 'tensor'), may hold values from -0.25 to 0.25
- key_weight: bfloat16 [3072, 4096], P(None, 'tensor'), may hold values from -2 to 2
- value_weight: bfloat16 [3072, 4096], P(None, 'tensor'), may hold values from -0.109375 to 0.109375
- output_weight: bfloat16 [4096, 3072], P('tensor'), may hold values from -1.25 to 1.25
- final_gain: float32 [3072], replicated, may hold values from 0.1 to 1.9
- reward_weight: float32 [3072], replicated, may hold values from -6 to 6
- token_ids: int32 [8192], P(('seq', 'tensor')), may hold values from 0 to 255999, as said below
- index_samples: float32 [8, 8, 8192], P(None, None, ('seq', 'tensor')), may hold values from -6 to 6
- feat_weight: float32 [3072, 256], replicated, may hold values from -0.109375 to 0.109375
- index_weight: float32 [8, 256], replicated, may hold values from -2 to 2
- first_bias: float32 [256], replicated, may hold values from -3 to 3
- middle_weight: float32 [256, 256], replicated, may hold values from -0.375 to 0.375
- second_bias: float32 [256], replicated, may hold values from -3 to 3
- head_weight: float32 [256, 8], replicated, may hold values from -0.375 to 0.375
- pair_ids: int32 [8, 2], replicated, may hold values from 0 to 15, all different within a row
Outputs:
- features: bfloat16 [8192, 3072], P(('seq', 'tensor'))
- pair_margin: float32 [8, 8], replicated
- grad_feature: float32 [3072, 256], P(('seq', 'tensor'))
- grad_index: float32 [8, 256], replicated
- grad_first: float32 [256], replicated
- grad_middle: float32 [256, 256], replicated
- grad_second: float32 [256], replicated
- grad_head: float32 [256, 8], replicated
Inputs may be any that keep to these rules, and one draw needn't show every extreme that they name: `token_ids`: in each response of 512 positions the positions before its last valid one hold ids from 2 to 255999, the last valid one holds 1 and the positions after it hold 0; every response has at least 128 valid tokens and at least one 0; the first position of the first response holds 255999. `pair_ids`: each row names two different responses, chosen first; every response stands in exactly one pair.
All inputs are finite; a program needn't handle non-finite values.
Results may differ from a plain program's by a relative error of at most 0.012.
The roundings to bfloat16 on the way count: a program that leaves them out, or rounds other values in their place, can miss the bound.
Values may be sent and summed in bfloat16 or wider, within the bound.
A program may use at most 128 MiB of HBM per device.

v0:
```python
import jax
import jax.numpy as jnp
from jax import lax
from jax.sharding import PartitionSpec as P

HEAD_DIM = 256
RESP_LEN = 512
norm_eps = 1e-06
rope_base = 10000.0
gelu_coef = 0.044715
gelu_root = 0.7978845608028654
masked_score = -1e30


def rms_scale(rows, gain):
    mean_square = jnp.mean(rows * rows, axis=-1, keepdims=True)
    return rows * lax.rsqrt(mean_square + norm_eps) * (1.0 + gain)


def rotate_pairs(entries, positions):
    half_dim = entries.shape[-1] // 2
    freqs = rope_base ** (-(jnp.arange(half_dim, dtype=jnp.float32) * 2.0) / entries.shape[-1])
    angles = positions.astype(jnp.float32)[:, None] * freqs[None, :]
    cosine = jnp.cos(angles)[:, None, :]
    sine = jnp.sin(angles)[:, None, :]
    first_half = entries[..., :half_dim]
    second_half = entries[..., half_dim:]
    return jnp.concatenate(
        [first_half * cosine - second_half * sine, second_half * cosine + first_half * sine],
        axis=-1,
    )


def gelu_tanh(inputs):
    return (
        0.5 * inputs * (1.0 + jnp.tanh(gelu_root * (inputs + gelu_coef * inputs * inputs * inputs)))
    )


def gelu_slope(inputs):
    tangent = jnp.tanh(gelu_root * (inputs + gelu_coef * inputs * inputs * inputs))
    inner_slope = gelu_root * (1.0 + 3.0 * gelu_coef * inputs * inputs)
    return 0.5 * (1.0 + tangent) + 0.5 * inputs * (1.0 - tangent * tangent) * inner_slope


def shards(
    hidden,
    norm_gain,
    query_weight,
    key_weight,
    value_weight,
    output_weight,
    final_gain,
    reward_weight,
    token_ids,
    index_samples,
    feat_weight,
    index_weight,
    first_bias,
    middle_weight,
    second_bias,
    head_weight,
    pair_ids,
):
    tp_count = lax.axis_size("tensor")
    tp_index = lax.axis_index("tensor")
    seq_index = lax.axis_index("seq")
    whole_rows = lax.all_gather(hidden, "tensor", axis=1, tiled=True)
    tok_seq = whole_rows.shape[0]
    width = whole_rows.shape[1]
    local_heads = query_weight.shape[1] // HEAD_DIM
    local_resp = tok_seq // RESP_LEN
    normed = rms_scale(whole_rows.astype(jnp.float32), norm_gain).astype(jnp.bfloat16)
    positions = jnp.arange(RESP_LEN, dtype=jnp.int32)
    causal = positions[None, :] <= positions[:, None]
    head_shape = (local_resp, RESP_LEN, local_heads, HEAD_DIM)
    queries = jnp.dot(normed, query_weight, preferred_element_type=jnp.float32).reshape(head_shape)
    queries = rotate_pairs(queries, positions).astype(jnp.bfloat16)
    key_rows = jnp.dot(normed, key_weight, preferred_element_type=jnp.float32).reshape(head_shape)
    key_rows = rotate_pairs(key_rows, positions).astype(jnp.bfloat16)
    value_rows = (
        jnp.dot(normed, value_weight, preferred_element_type=jnp.float32)
        .astype(jnp.bfloat16)
        .reshape(head_shape)
    )
    scores = jnp.einsum(
        "rqhd,rkhd->rhqk", queries, key_rows, preferred_element_type=jnp.float32
    ) * HEAD_DIM ** (-0.5)
    scores = jnp.where(causal[None, None, :, :], scores, masked_score)
    highest = jnp.max(scores, axis=-1, keepdims=True)
    weights = jnp.exp(scores - highest)
    probs = (weights / jnp.sum(weights, axis=-1, keepdims=True)).astype(jnp.bfloat16)
    attended = jnp.einsum(
        "rhqk,rkhd->rqhd", probs, value_rows, preferred_element_type=jnp.float32
    ).astype(jnp.bfloat16)
    attended = attended.reshape(tok_seq, local_heads * HEAD_DIM)
    partial_out = jnp.dot(attended, output_weight, preferred_element_type=jnp.float32)
    mixed = lax.psum_scatter(partial_out, "tensor", scatter_dimension=1, tiled=True)
    local_width = mixed.shape[1]
    summed = hidden.astype(jnp.float32) + mixed
    square_sums = lax.psum(jnp.sum(summed * summed, axis=1), "tensor")
    gain_part = lax.dynamic_slice_in_dim(final_gain, tp_index * local_width, local_width, 0)
    local_feat = (
        summed * lax.rsqrt(square_sums[:, None] / width + norm_eps) * (1.0 + gain_part)
    ).astype(jnp.bfloat16)
    features = lax.all_to_all(local_feat, "tensor", split_axis=0, concat_axis=1, tiled=True)
    feat32 = features.astype(jnp.float32)
    tok_epi = feat32.shape[0]
    base = jnp.dot(feat32, reward_weight, precision=lax.Precision.HIGHEST)
    feat_part = jnp.dot(feat32, feat_weight, precision=lax.Precision.HIGHEST)
    index_part = jnp.einsum(
        "sit,ie->ste", index_samples, index_weight, precision=lax.Precision.HIGHEST
    )
    first_pre = feat_part[None, :, :] + index_part + first_bias
    first_act = gelu_tanh(first_pre)
    second_pre = (
        jnp.einsum("ste,ef->stf", first_act, middle_weight, precision=lax.Precision.HIGHEST)
        + second_bias
    )
    second_act = gelu_tanh(second_pre)
    head_out = jnp.einsum("ste,ei->sti", second_act, head_weight, precision=lax.Precision.HIGHEST)
    epinet_out = jnp.einsum("sti,sit->st", head_out, index_samples, precision=lax.Precision.HIGHEST)
    resp_total = 2 * pair_ids.shape[0]
    first_token = (seq_index * tp_count + tp_index) * tok_epi
    token_pos = first_token + jnp.arange(tok_epi, dtype=jnp.int32)
    owner = token_pos // RESP_LEN
    slot_ids = jnp.arange(resp_total, dtype=jnp.int32)
    owner_table = (owner[:, None] == slot_ids[None, :]).astype(jnp.float32)
    valid = (token_ids != 0).astype(jnp.float32)
    part_totals = jnp.dot(
        (base[None, :] + epinet_out) * valid[None, :], owner_table, precision=lax.Precision.HIGHEST
    )
    part_counts = jnp.dot(valid, owner_table, precision=lax.Precision.HIGHEST)
    totals, counts = lax.psum((part_totals, part_counts), ("seq", "tensor"))
    means = totals / counts[None, :]
    sign_table = (pair_ids[:, 0:1] == slot_ids[None, :]).astype(jnp.float32) - (
        pair_ids[:, 1:2] == slot_ids[None, :]
    ).astype(jnp.float32)
    margin = jnp.dot(means, sign_table.T, precision=lax.Precision.HIGHEST)
    pair_margin = margin.T
    margin_grad = -jax.nn.sigmoid(-margin)
    mean_grad = jnp.dot(margin_grad, sign_table, precision=lax.Precision.HIGHEST) / counts[None, :]
    reward_grad = (
        jnp.dot(mean_grad, owner_table.T, precision=lax.Precision.HIGHEST) * valid[None, :]
    )
    out_grad = jnp.einsum("st,sit->sti", reward_grad, index_samples)
    grad_head = jnp.einsum("ste,sti->ei", second_act, out_grad, precision=lax.Precision.HIGHEST)
    second_grad = jnp.einsum(
        "sti,ei->ste", out_grad, head_weight, precision=lax.Precision.HIGHEST
    ) * gelu_slope(second_pre)
    grad_second = jnp.sum(second_grad, axis=(0, 1))
    grad_middle = jnp.einsum("ste,stf->ef", first_act, second_grad, precision=lax.Precision.HIGHEST)
    first_grad = jnp.einsum(
        "stf,ef->ste", second_grad, middle_weight, precision=lax.Precision.HIGHEST
    ) * gelu_slope(first_pre)
    grad_first = jnp.sum(first_grad, axis=(0, 1))
    grad_index = jnp.einsum(
        "sit,ste->ie", index_samples, first_grad, precision=lax.Precision.HIGHEST
    )
    feat_grad = jnp.sum(first_grad, axis=0)
    grad_feature = lax.psum_scatter(
        jnp.einsum("td,te->de", feat32, feat_grad, precision=lax.Precision.HIGHEST),
        ("seq", "tensor"),
        scatter_dimension=0,
        tiled=True,
    )
    summed_grads = lax.psum(
        (grad_index, grad_first, grad_middle, grad_second, grad_head), ("seq", "tensor")
    )
    return (
        features,
        pair_margin,
        grad_feature,
        summed_grads[0],
        summed_grads[1],
        summed_grads[2],
        summed_grads[3],
        summed_grads[4],
    )


def solution(mesh):
    return jax.shard_map(
        shards,
        mesh=mesh,
        in_specs=(
            P("seq", "tensor"),
            P(),
            P(None, "tensor"),
            P(None, "tensor"),
            P(None, "tensor"),
            P("tensor", None),
            P(),
            P(),
            P(("seq", "tensor")),
            P(None, None, ("seq", "tensor")),
            P(),
            P(),
            P(),
            P(),
            P(),
            P(),
            P(),
        ),
        out_specs=(
            P(("seq", "tensor"), None),
            P(),
            P(("seq", "tensor"), None),
            P(),
            P(),
            P(),
            P(),
            P(),
        ),
        check_vma=False,
    )
```

profile of v0, /device:TPU:0, one launch (start us, length us, event | category | flops | bytes accessed | tf_op | source)
XLA Modules:
  0.0 796.9 jit_solution(2931273031737406126)
XLA Ops:
  11.2 116.4 %all-gather.2.cloned.1.call-done = bf16[1024,3072]{1,0:T(8,128)(2,1)} async-done(((bf16[1024,768]{1,0:T(8,128)(2,1)}), bf16[1024,3072]{1,0:T(8,128)(2,1)}) %all-gather.2.cloned.1.call-update) | async-done | bytes 6291472 | tf_op jit(solution)/shard_map/all_gather | solution.py:68
  127.7 4.2 fusion.1
  132.3 9.9 %convolution_convert_fusion = bf16[1024,1024]{1,0:T(8,128)(2,1)} fusion(bf16[3072,1024]{1,0:T(8,128)(2,1)} %param.21, bf16[1024,3072]{1,0:T(8,128)(2,1)S(1)} %copy-done.2, f32[3072]{0:T(1024)S(1)} %broadcast_add_fusion, f32[1024]{0:T(1024)S(1)} %add_rsqrt_fusion.1), kind=kOutput, calls=%fused_computation.51 | convolution fusion | flops 6456082432 | bytes 14696448 | tf_op jit(solution)/shard_map/dot_general | solution.py:82
  142.2 4.5 reshape.148
  146.7 12.1 %fusion.86 = f32[1024,1024]{1,0:T(8,128)} fusion(bf16[3072,1024]{1,0:T(8,128)(2,1)} %param.20, bf16[1024,3072]{1,0:T(8,128)(2,1)} %all-gather.2.cloned.1.call-done, f32[3072]{0:T(1024)S(1)} %broadcast_add_fusion, f32[1024]{0:T(1024)S(1)} %add_rsqrt_fusion.1), kind=kOutput, calls=%fused_computation.132 | convolution fusion | flops 6455033856 | bytes 16793600 | tf_op jit(solution)/shard_map/dot_general | solution.py:79
  158.9 5.6 reshape.150
  164.5 12.1 %fusion.88 = f32[1024,1024]{1,0:T(8,128)} fusion(bf16[3072,1024]{1,0:T(8,128)(2,1)} %param.19, bf16[1024,3072]{1,0:T(8,128)(2,1)} %all-gather.2.cloned.1.call-done, f32[3072]{0:T(1024)S(1)} %broadcast_add_fusion, f32[1024]{0:T(1024)S(1)} %add_rsqrt_fusion.1), kind=kOutput, calls=%fused_computation.133 | convolution fusion | flops 6455033856 | bytes 16793600 | tf_op jit(solution)/shard_map/dot_general | solution.py:77
  176.6 5.8 reshape.149
  182.4 4.1 fusion.93
  189.1 5.6 fusion.95
  194.8 6.1 convert_bitcast_fusion
  200.8 4.2 copy.40
  205.1 2.1 copy.56
  207.2 12.3 %fusion.97 = f32[1024,3072]{1,0:T(8,128)} fusion(bf16[1024,1024]{1,0:T(8,128)(2,1)S(1)} %bitcast.76, bf16[1024,3072]{1,0:T(8,128)(2,1)} %param.22), kind=kOutput, calls=%fused_computation.140 | convolution fusion | flops 6442450944 | bytes 20971520 | tf_op jit(solution)/shard_map/dot_general | solution.py:97
  220.3 209.4 %reduce-scatter.3.cloned.1.call-done = f32[1024,768]{1,0:T(8,128)} async-done(((f32[1024,3072]{1,0:T(8,128)}), f32[1024,768]{1,0:T(8,128)}) %reduce-scatter.3.cloned.1.call-update) | async-done | bytes 3145744 | tf_op jit(solution)/shard_map/reduce_scatter | solution.py:98
  429.7 2.8 multiply_reduce_fusion
  432.6 11.5 %psum.56 = f32[1024]{0:T(1024)S(1)} all-reduce(f32[1024]{0:T(1024)S(1)} %multiply_reduce_fusion), channel_id=1, replica_groups=mesh['seq'=8,'tensor'=4] {'tensor'}, use_global_device_ids=true, to_apply=%region_5.6 | all-reduce | flops 1024 | bytes 8192 | tf_op jit(solution)/shard_map/psum | solution.py:101
  444.0 4.0 multiply_convert_fusion
  448.0 4.5 all-to-all-start
  453.1 35.0 %all-to-all-done = bf16[4,256,768]{2,1,0:T(8,128)(2,1)} async-done(((bf16[4,256,768]{2,1,0:T(8,128)(2,1)}), bf16[4,256,768]{2,1,0:T(8,128)(2,1)}, u32[]{:S(2)}, u32[]{:S(2)}) %all-to-all-start) | async-done | bytes 1572896 | tf_op jit(solution)/shard_map/all_to_all | solution.py:106
  492.8 2.0 add_add_fusion
  494.8 2.3 fusion.34
  497.2 2.5 fusion.33
  500.0 38.3 %all-reduce.1 = (f32[8,16]{1,0:T(8,128)S(1)}, f32[16]{0:T(128)S(1)}) all-reduce(f32[8,16]{1,0:T(8,128)S(1)} %fusion.37, f32[16]{0:T(128)S(1)} %convolution_bitcast_fusion.3), channel_id=1, replica_groups=mesh['seq'=8,'tensor'=4] {'seq','tensor'}, use_global_device_ids=true, to_apply=%region_6.7 | all-reduce | flops 144 | bytes 1152 | tf_op jit(solution)/shard_map/psum | solution.py:134
  538.9 4.9 fusion.96
  545.3 4.6 convolution_bitcast_fusion
  549.9 6.6 fusion.91
  556.8 4.8 fusion.100
  562.3 2.8 convolution_bitcast_fusion.2
  566.9 41.8 %all-reduce = (f32[8,256]{1,0:T(8,128)}, f32[256]{0:T(256)}, f32[256]{0:T(256)}, f32[256,8]{0,1:T(8,128)}) all-reduce(f32[8,256]{1,0:T(8,128)S(1)} %convolution_bitcast_fusion.2, f32[256]{0:T(256)S(1)} %get-tuple-element.24, f32[256]{0:T(256)S(1)} %get-tuple-element.51, ...), channel_id=1, replica_groups=mesh['seq'=8,'tensor'=4] {'seq','tensor'}, use_global_device_ids=true, to_apply=%region_10.11 | all-reduce | flops 4608 | bytes 36864 | tf_op jit(solution)/shard_map/psum | solution.py:167
  608.7 73.4 %all-reduce.4.cloned.1.call-done = f32[256,256]{1,0:T(8,128)} async-done(((f32[256,256]{1,0:T(8,128)}), f32[256,256]{1,0:T(8,128)}) %all-reduce.4.cloned.1.call-update) | async-done | bytes 262160 | tf_op jit(solution)/shard_map/psum | solution.py:167
  682.1 106.4 %reduce-scatter.5.cloned.1.call-done = f32[96,256]{1,0:T(8,128)} async-done(((f32[3072,256]{1,0:T(8,128)}), f32[96,256]{1,0:T(8,128)}) %reduce-scatter.5.cloned.1.call-update) | async-done | bytes 98320 | tf_op jit(solution)/shard_map/reduce_scatter | solution.py:161
  (73 shorter events, 19.6 us)
Async XLA Ops:
  7.2 483.8 %copy-start = (f32[3072,256]{1,0:T(8,128)S(1)}, f32[3072,256]{1,0:T(8,128)}, u32[]{:S(2)}) copy-start(f32[3072,256]{1,0:T(8,128)} %param.27) | copy-start | bytes 9437188
  7.2 120.5 %all-gather.2.cloned.1.call-start = ((), (), s32[]{:S(2)}) async-start(), calls=%async_computation.3 | async-start | bytes 7864320 | tf_op jit(solution)/shard_map/all_gather | solution.py:68
  7.9 421.8 %reduce-scatter.3.cloned.1.call-start = ((), (), s32[]{:S(2)}) async-start(), calls=%async_computation.4 | async-start | bytes 15728640 | tf_op jit(solution)/shard_map/reduce_scatter | solution.py:98
  127.7 4.6 copy-start.2
  182.4 4.2 copy-start.6
  187.8 1.3 copy-start.8
  189.1 5.6 copy-start.3
  448.0 4.8 copy-start.12
  448.0 5.0 copy-start.13
  448.0 40.0 %all-to-all-start = ((bf16[4,256,768]{2,1,0:T(8,128)(2,1)}), bf16[4,256,768]{2,1,0:T(8,128)(2,1)}, u32[]{:S(2)}, u32[]{:S(2)}) async-start(bf16[4,256,768]{2,1,0:T(8,128)(2,1)} %bitcast.75), calls=%async_computation.1 | async-start | bytes 3145728 | tf_op jit(solution)/shard_map/all_to_all | solution.py:106
  452.5 37.1 %copy-start.9 = (f32[3072]{0:T(1024)S(1)}, f32[3072]{0:T(1024)}, u32[]{:S(2)}) copy-start(f32[3072]{0:T(1024)} %param.24) | copy-start | bytes 36868
  452.5 229.6 %all-reduce.4.cloned.1.call-start = ((), (), s32[]{:S(2)}) async-start(), calls=%async_computation.6 | async-start | bytes 524288 | tf_op jit(solution)/shard_map/psum | solution.py:167
  489.6 3.2 copy-start.1
  491.0 1.8 copy-start.7
  491.0 1.8 copy-start.10
  491.0 1.8 copy-start.11
  492.8 2.0 copy-start.14
  494.8 2.4 copy-start.4
  494.8 2.4 copy-start.15
  494.8 2.4 copy-start.16
  497.2 2.6 copy-start.17
  538.9 6.3 copy-start.5
  543.9 1.4 copy-start.19
  556.6 231.9 %reduce-scatter.5.cloned.1.call-start = ((), (), s32[]{:S(2)}) async-start(), calls=%async_computation.5 | async-start | bytes 3244032 | tf_op jit(solution)/shard_map/reduce_scatter | solution.py:161
  562.3 2.8 copy-start.18
Sparse Core Ops, SparseCore 0:
  9.6 118.0 all-gather.1
  219.6 210.0 reduce-scatter.2
  556.7 125.3 all-reduce.3
  688.0 100.4 reduce-scatter.4
where the time goes:
time: 806 us; the launch traced here: 797 us
  waiting for transfers between devices  541 us (67%)
  blocking collectives  91.6 us (11%)
  matrix products  90.4 us (11%)
  local copies, waits for them, and re-layouts  32.2 us (4%)
  other arithmetic  22 us (3%)
  between operations  14.3 us (2%)
    reduce_scatter x1, waiting for transfers between devices, shards(): lax.psum_scatter(partial_out, 'tensor', scatter_dimension=1, tiled=True)  209 us
    all_gather x1, waiting for transfers between devices, shards(): whole_rows = lax.all_gather(hidden, 'tensor', axis=1, tiled=True)  116 us
    reduce_scatter x1, waiting for transfers between devices, shards(): lax.psum_scatter(jnp.einsum('td,te->de', feat32, feat_grad, precision=lax...  106 us
    psum x1, waiting for transfers between devices, shards(): lax.psum((grad_index, grad_first, grad_middle, grad_second, grad_head), (...  73.4 us
    psum x1, blocking collectives, shards(): lax.psum((grad_index, grad_first, grad_middle, grad_second, grad_head), (...  41.8 us
    psum x1, blocking collectives, shards(): totals, counts = lax.psum((part_totals, part_counts), ('seq', 'tensor'))  38.3 us
    all_to_all x1, waiting for transfers between devices, shards(): lax.all_to_all(local_feat, 'tensor', split_axis=0, concat_axis=1, tiled=T...  35 us
  transfers between devices with their start and end apart: 5, of which 5 were waited for; matrix products, arithmetic and copies ran while one was open for 2% of the time, Pallas kernels for 0%

commit v1 on v0

--- a/solution.py
+++ b/solution.py
@@ -103,7 +103,12 @@
     local_feat = (
         summed * lax.rsqrt(square_sums[:, None] / width + norm_eps) * (1.0 + gain_part)
     ).astype(jnp.bfloat16)
-    features = lax.all_to_all(local_feat, "tensor", split_axis=0, concat_axis=1, tiled=True)
+    features = jnp.concatenate(
+        lax.all_to_all(
+            jnp.stack(jnp.split(local_feat, lax.axis_size("tensor"), axis=0)), "tensor", 0, 0
+        ),
+        axis=1,
+    )
     feat32 = features.astype(jnp.float32)
     tok_epi = feat32.shape[0]
     base = jnp.dot(feat32, reward_weight, precision=lax.Precision.HIGHEST)

time: 806 us -> 809 us (level)
  no operation moved by 1% of the time
where the time goes in v1:
time: 809 us; the launch traced here: 800 us
  waiting for transfers between devices  539 us (67%)
  blocking collectives  91.7 us (11%)
  matrix products  91.4 us (11%)
  local copies, waits for them, and re-layouts  36 us (4%)
  other arithmetic  22.2 us (3%)
  between operations  14.3 us (2%)
    reduce_scatter x1, waiting for transfers between devices, shards(): lax.psum_scatter(partial_out, 'tensor', scatter_dimension=1, tiled=True)  209 us
    all_gather x1, waiting for transfers between devices, shards(): whole_rows = lax.all_gather(hidden, 'tensor', axis=1, tiled=True)  116 us
    reduce_scatter x1, waiting for transfers between devices, shards(): lax.psum_scatter(jnp.einsum('td,te->de', feat32, feat_grad, precision=lax...  106 us
    psum x1, waiting for transfers between devices, shards(): lax.psum((grad_index, grad_first, grad_middle, grad_second, grad_head), (...  71.3 us
    psum x1, blocking collectives, shards(): lax.psum((grad_index, grad_first, grad_middle, grad_second, grad_head), (...  41.9 us
    psum x1, blocking collectives, shards(): totals, counts = lax.psum((part_totals, part_counts), ('seq', 'tensor'))  38.3 us
    all_to_all x1, waiting for transfers between devices, shards(): lax.all_to_all(jnp.stack(jnp.split(local_feat, lax.axis_size('tensor'), a...  35.1 us
  transfers between devices with their start and end apart: 5, of which 5 were waited for; matrix products, arithmetic and copies ran while one was open for 2% of the time, Pallas kernels for 0%

profile of v1, /device:TPU:0, one launch (start us, length us, event | category | flops | bytes accessed | tf_op | source)
XLA Modules:
  0.0 799.8 jit_solution(11612607930272050264)
XLA Ops:
  11.2 116.4 %all-gather.2.cloned.1.call-done = bf16[1024,3072]{1,0:T(8,128)(2,1)} async-done(((bf16[1024,768]{1,0:T(8,128)(2,1)}), bf16[1024,3072]{1,0:T(8,128)(2,1)}) %all-gather.2.cloned.1.call-update) | async-done | bytes 6291472 | tf_op jit(solution)/shard_map/all_gather | solution.py:68
  127.7 4.2 fusion.1
  132.3 9.9 %convolution_convert_fusion = bf16[1024,1024]{1,0:T(8,128)(2,1)} fusion(bf16[3072,1024]{1,0:T(8,128)(2,1)} %param.21, bf16[1024,3072]{1,0:T(8,128)(2,1)S(1)} %copy-done.2, f32[3072]{0:T(1024)S(1)} %broadcast_add_fusion, f32[1024]{0:T(1024)S(1)} %add_rsqrt_fusion.1), kind=kOutput, calls=%fused_computation.51 | convolution fusion | flops 6456082432 | bytes 14696448 | tf_op jit(solution)/shard_map/dot_general | solution.py:82
  142.2 4.5 reshape.151
  146.7 12.1 %fusion.86 = f32[1024,1024]{1,0:T(8,128)} fusion(bf16[3072,1024]{1,0:T(8,128)(2,1)} %param.20, bf16[1024,3072]{1,0:T(8,128)(2,1)} %all-gather.2.cloned.1.call-done, f32[3072]{0:T(1024)S(1)} %broadcast_add_fusion, f32[1024]{0:T(1024)S(1)} %add_rsqrt_fusion.1), kind=kOutput, calls=%fused_computation.137 | convolution fusion | flops 6455033856 | bytes 16793600 | tf_op jit(solution)/shard_map/dot_general | solution.py:79
  158.8 5.6 reshape.153
  164.4 12.1 %fusion.88 = f32[1024,1024]{1,0:T(8,128)} fusion(bf16[3072,1024]{1,0:T(8,128)(2,1)} %param.19, bf16[1024,3072]{1,0:T(8,128)(2,1)} %all-gather.2.cloned.1.call-done, f32[3072]{0:T(1024)S(1)} %broadcast_add_fusion, f32[1024]{0:T(1024)S(1)} %add_rsqrt_fusion.1), kind=kOutput, calls=%fused_computation.138 | convolution fusion | flops 6455033856 | bytes 16793600 | tf_op jit(solution)/shard_map/dot_general | solution.py:77
  176.6 5.8 reshape.152
  182.4 4.1 fusion.93
  189.1 5.6 fusion.95
  194.8 6.1 convert_bitcast_fusion
  200.8 4.2 copy.39
  207.1 12.3 %fusion.97 = f32[1024,3072]{1,0:T(8,128)} fusion(bf16[1024,1024]{1,0:T(8,128)(2,1)S(1)} %bitcast.81, bf16[1024,3072]{1,0:T(8,128)(2,1)} %param.22), kind=kOutput, calls=%fused_computation.145 | convolution fusion | flops 6442450944 | bytes 20971520 | tf_op jit(solution)/shard_map/dot_general | solution.py:97
  220.3 209.4 %reduce-scatter.3.cloned.1.call-done = f32[1024,768]{1,0:T(8,128)} async-done(((f32[1024,3072]{1,0:T(8,128)}), f32[1024,768]{1,0:T(8,128)}) %reduce-scatter.3.cloned.1.call-update) | async-done | bytes 3145744 | tf_op jit(solution)/shard_map/reduce_scatter | solution.py:98
  429.7 2.8 multiply_reduce_fusion
  432.5 11.5 %psum.56 = f32[1024]{0:T(1024)S(1)} all-reduce(f32[1024]{0:T(1024)S(1)} %multiply_reduce_fusion), channel_id=1, replica_groups=mesh['seq'=8,'tensor'=4] {'tensor'}, use_global_device_ids=true, to_apply=%region_5.6 | all-reduce | flops 1024 | bytes 8192 | tf_op jit(solution)/shard_map/psum | solution.py:101
  444.0 2.8 multiply_convert_fusion
  448.3 4.5 all-to-all-start
  453.1 35.1 %all-to-all-done = bf16[4,256,768]{2,1,0:T(8,128)(2,1)} async-done(((bf16[4,256,768]{2,1,0:T(8,128)(2,1)}), bf16[4,256,768]{2,1,0:T(8,128)(2,1)}, u32[]{:S(2)}, u32[]{:S(2)}) %all-to-all-start) | async-done | bytes 1572896 | tf_op jit(solution)/shard_map/all_to_all | solution.py:107
  488.3 2.8 copy.40
  497.6 2.3 fusion.34
  500.0 2.5 fusion.33
  502.8 38.3 %all-reduce.1 = (f32[8,16]{1,0:T(8,128)S(1)}, f32[16]{0:T(128)S(1)}) all-reduce(f32[8,16]{1,0:T(8,128)S(1)} %fusion.37, f32[16]{0:T(128)S(1)} %convolution_bitcast_fusion.3), channel_id=1, replica_groups=mesh['seq'=8,'tensor'=4] {'seq','tensor'}, use_global_device_ids=true, to_apply=%region_6.7 | all-reduce | flops 144 | bytes 1152 | tf_op jit(solution)/shard_map/psum | solution.py:139
  541.7 4.9 fusion.96
  548.1 4.6 convolution_bitcast_fusion
  552.7 6.6 fusion.91
  559.6 4.5 fusion.100
  564.1 2.6 copy.42
  567.3 2.8 convolution_bitcast_fusion.2
  571.9 41.9 %all-reduce = (f32[8,256]{1,0:T(8,128)}, f32[256]{0:T(256)}, f32[256]{0:T(256)}, f32[256,8]{0,1:T(8,128)}) all-reduce(f32[8,256]{1,0:T(8,128)S(1)} %convolution_bitcast_fusion.2, f32[256]{0:T(256)S(1)} %get-tuple-element.24, f32[256]{0:T(256)S(1)} %get-tuple-element.55, ...), channel_id=1, replica_groups=mesh['seq'=8,'tensor'=4] {'seq','tensor'}, use_global_device_ids=true, to_apply=%region_10.11 | all-reduce | flops 4608 | bytes 36864 | tf_op jit(solution)/shard_map/psum | solution.py:172
  613.8 71.3 %all-reduce.4.cloned.1.call-done = f32[256,256]{1,0:T(8,128)} async-done(((f32[256,256]{1,0:T(8,128)}), f32[256,256]{1,0:T(8,128)}) %all-reduce.4.cloned.1.call-update) | async-done | bytes 262160 | tf_op jit(solution)/shard_map/psum | solution.py:172
  685.0 106.4 %reduce-scatter.5.cloned.1.call-done = f32[96,256]{1,0:T(8,128)} async-done(((f32[3072,256]{1,0:T(8,128)}), f32[96,256]{1,0:T(8,128)}) %reduce-scatter.5.cloned.1.call-update) | async-done | bytes 98320 | tf_op jit(solution)/shard_map/reduce_scatter | solution.py:166
  (76 shorter events, 24.6 us)
Async XLA Ops:
  7.2 486.1 %copy-start = (f32[3072,256]{1,0:T(8,128)S(1)}, f32[3072,256]{1,0:T(8,128)}, u32[]{:S(2)}) copy-start(f32[3072,256]{1,0:T(8,128)} %param.27) | copy-start | bytes 9437188
  7.2 120.5 %all-gather.2.cloned.1.call-start = ((), (), s32[]{:S(2)}) async-start(), calls=%async_computation.3 | async-start | bytes 7864320 | tf_op jit(solution)/shard_map/all_gather | solution.py:68
  7.9 421.8 %reduce-scatter.3.cloned.1.call-start = ((), (), s32[]{:S(2)}) async-start(), calls=%async_computation.4 | async-start | bytes 15728640 | tf_op jit(solution)/shard_map/reduce_scatter | solution.py:98
  127.7 4.6 copy-start.2
  182.4 4.2 copy-start.6
  187.8 1.3 copy-start.8
  189.1 5.6 copy-start.3
  448.3 4.6 copy-start.12
  448.3 4.8 copy-start.13
  448.3 40.0 %all-to-all-start = ((bf16[4,256,768]{2,1,0:T(8,128)(2,1)}), bf16[4,256,768]{2,1,0:T(8,128)(2,1)}, u32[]{:S(2)}, u32[]{:S(2)}) async-start(bf16[4,256,768]{2,1,0:T(8,128)(2,1)} %pad_maximum_fusion), calls=%async_computation.1 | async-start | bytes 3145728 | tf_op jit(solution)/shard_map/all_to_all | solution.py:107
  452.8 38.3 %copy-start.9 = (f32[3072]{0:T(1024)S(1)}, f32[3072]{0:T(1024)}, u32[]{:S(2)}) copy-start(f32[3072]{0:T(1024)} %param.24) | copy-start | bytes 36868
  452.8 232.2 %all-reduce.4.cloned.1.call-start = ((), (), s32[]{:S(2)}) async-start(), calls=%async_computation.6 | async-start | bytes 524288 | tf_op jit(solution)/shard_map/psum | solution.py:172
  491.1 2.3 copy-start.1
  493.3 2.2 copy-start.7
  493.3 2.2 copy-start.10
  493.3 2.2 copy-start.11
  495.6 2.0 copy-start.14
  497.6 2.4 copy-start.4
  497.6 2.4 copy-start.15
  497.6 2.4 copy-start.16
  500.0 2.6 copy-start.17
  541.7 6.3 copy-start.5
  546.7 1.4 copy-start.19
  559.4 232.1 %reduce-scatter.5.cloned.1.call-start = ((), (), s32[]{:S(2)}) async-start(), calls=%async_computation.5 | async-start | bytes 3244032 | tf_op jit(solution)/shard_map/reduce_scatter | solution.py:166
  567.3 2.8 copy-start.18
Sparse Core Ops, SparseCore 0:
  9.6 118.0 all-gather.1
  219.6 210.0 reduce-scatter.2
  559.5 125.5 all-reduce.3
  690.9 100.4 reduce-scatter.4
